TPU v7x, 32 devices: a whole 2x2x4 slice. The times are simulated.
32 devices in a mesh: groups: 2 (over y), rows: 8 (over z, x), cols: 2 (over core).
Axes of the slice: x: 2, y: 2, z: 4, core: 2. Of those that a mesh axis runs over, the one named last changes fastest.
Arguments:
- earlier_features: bfloat16 [64, 96, 1024], P(('groups', 'rows', 'cols')), parts along dimension 0, may hold values from -6 to 6
- later_features: bfloat16 [64, 96, 1024], P(('groups', 'rows', 'cols')), parts along dimension 0, may hold values from -6 to 6
- cotangent: bfloat16 [64, 128, 1024], P(('groups', 'rows', 'cols')), parts along dimension 0, may hold values from -6 to 6
- proj_weight: bfloat16 [162, 128], replicated, may hold values from -0.5 to 0.5
- owner_slot: int32 [64], P('groups'), parts along dimension 0, may hold values from 0 to 31, as said below
- neighbour_labels: int32 [64, 8], P(('groups', 'rows', 'cols')), parts along dimension 0, may hold values from -1 to 31, as said below
- disk_mask: int32 [64], P(('groups', 'rows', 'cols')), parts along dimension 0, may hold values from 0 to 1, as said below
Outputs:
- flow_features: bfloat16 [64, 128, 1024], P(('groups', 'rows', 'cols')), parts along dimension 0
- grad_first: bfloat16 [64, 96, 1024], P(('groups', 'rows', 'cols')), parts along dimension 0
- grad_second: bfloat16 [64, 96, 1024], P(('groups', 'rows', 'cols')), parts along dimension 0
- grad_proj: float32 [324, 128], P('groups'), parts along dimension 0
There are 2 independent parts, one for each index of `groups`. A program takes and returns all parts, laid end to end along the dimension named above; an argument that names none is the same for every part. Nothing has to cross between parts.
Inputs may be any that keep to these rules, and one draw needn't show every extreme that they name: A permutation: owner_slot[l] is the slot holding the tile labelled l. The tiles form a grid of 8 rows by 4 columns; the device at rows index r and cols index c holds slots (2 * r + c) * 2 to (2 * r + c + 1) * 2 - 1, which carry tile row r and tile columns c * 2 to (c + 1) * 2 - 1 in an order of their own. `neighbour_labels`: for slot s and direction j, the label of the tile one step away in that direction on the tile grid, or -1 where that tile is outside the grid or off the disk. `disk_mask`: 1 where the slot's tile lies on the disk, a single circle over the tile grid; 0 elsewhere.
All inputs are finite; a program needn't handle non-finite values.
Results may differ from a plain program's by a relative error of at most 0.0049.
Values may be sent and summed in bfloat16 or wider, within the bound.
A program may use at most 256 MiB of HBM per device.

v0:
```python
import math

import jax
import jax.numpy as jnp
from jax import lax
from jax.experimental import pallas as pl
from jax.experimental.pallas import tpu as pltpu
from jax.sharding import PartitionSpec as P

CHANNELS = 96
WIDTH = 128
GRID = 16
STRIP = 32
MARGIN = 4
WINDOW = 9
PITCH = 48
LANES = 512
EXT_ROWS = (GRID - 1) * PITCH + LANES
SCALE = 1.0 / math.sqrt(CHANNELS)
F32 = jnp.float32
BF16 = jnp.bfloat16
NT = (((1,), (1,)), ((), ()))
NN = (((1,), (0,)), ((), ()))
TN = (((0,), (0,)), ((), ()))


def dot(a, b, dims):
    return lax.dot_general(a, b, dims, preferred_element_type=F32)


def permutation(backwards):
    o = lax.broadcasted_iota(jnp.int32, (256, 256), 0)
    i = lax.broadcasted_iota(jnp.int32, (256, 256), 1)
    y = 2 * ((o >> 4) & 3) + (o >> 7)
    col = 15 - (o & 15) if backwards else o & 15
    x = 2 * col + ((o >> 6) & 1)
    return jnp.where(i == y * 32 + x, 1.0, 0.0).astype(BF16)


def left_slot(owner_ref, labels_ref):
    base = (lax.axis_index("rows") * lax.axis_size("cols") + lax.axis_index("cols")) * 2
    right_of = labels_ref[0, 3]
    left_of = labels_ref[1, 2]
    first = (right_of >= 0) & (owner_ref[jnp.maximum(right_of, 0)] == base + 1)
    second = (left_of >= 0) & (owner_ref[jnp.maximum(left_of, 0)] == base)
    return jnp.where(first | second, 0, 1)


def strip_rows(blk, row, half):
    return pl.ds((blk * 4 + row) * STRIP + half * 16, 16)


def split_kernel(owner, labels, mask, perm, earlier, later, cot, q_out, e_out, c_out, q_back, c_back, side, upc, downc):
    left = left_slot(owner, labels)
    col = lax.axis_index("cols")
    for half in range(2):
        slot = left if half == 0 else 1 - left
        keep = mask[slot].astype(F32)
        for blk in range(4):
            cols = slice(blk * 256, blk * 256 + 256)
            for src, dst, masked, order in (
                (earlier, q_out, True, 0),
                (later, e_out, True, 0),
                (cot, c_out, False, 0),
                (earlier, q_back, True, 1),
                (cot, c_back, False, 1),
            ):
                at = half ^ order
                tile = src[slot, :, cols]
                if src is not cot:
                    tile = jnp.concatenate([tile, jnp.zeros((WIDTH - CHANNELS, 256), BF16)], axis=0)
                v = dot(perm[order], tile, NT)
                if masked:
                    v = v * keep
                w = v.astype(BF16)
                for k in range(4):
                    for row in range(4):
                        r = k * 64 + row * 16
                        dst[k, strip_rows(blk, row, at), :] = w[r : r + 16]
                if src is not later:
                    s = v[:64] + v[64:128] + v[128:192] + v[192:]
                    if masked:
                        s = s * 0.25
                    s = s.astype(BF16)
                    for row in range(4):
                        dst[4, strip_rows(blk, row, at), :] = s[row * 16 : row * 16 + 16]
    sub = lax.broadcasted_iota(jnp.int32, (16, WIDTH), 0)
    edge = jnp.where(col == 0, (sub >= 12).astype(F32), (sub < 4).astype(F32)).astype(BF16)
    for k in range(4):
        for row in range(GRID):
            lo = e_out[k, row * STRIP : row * STRIP + 16, :]
            hi = e_out[k, row * STRIP + 16 : row * STRIP + 32, :]
            v = jnp.where(col == 0, hi, lo) * edge
            side[k, row * 16 : row * 16 + 16, :] = v
            if row < MARGIN:
                upc[k, row * 16 : row * 16 + 16, :] = v
            if row >= GRID - MARGIN:
                downc[k, (row - 12) * 16 : (row - 12) * 16 + 16, :] = v


def ext_row(row):
    return pl.multiple_of(row * PITCH, 16)


def forward_kernel(perm, w_ref, q, e, above, below, side, above_side, below_side, c, left_ref,
                   ext, flow, proj, skew, flow_t, coarse):
    col = lax.axis_index("cols")
    ext[...] = jnp.zeros_like(ext)
    for k in range(4):
        for row in range(GRID + 2 * MARGIN):
            if row < MARGIN:
                src, sd, at = above, above_side, row
            elif row < GRID + MARGIN:
                src, sd, at = e, side, row - MARGIN
            else:
                src, sd, at = below, below_side, row - GRID - MARGIN
            ext[k, 16 + row * PITCH : 16 + row * PITCH + 32, :] = src[k, at * STRIP : at * STRIP + 32, :]
            ext[k, pl.ds(ext_row(row + 1 - col), 16), :] = sd[k, at * 16 : at * 16 + 16, :]
    for i in range(0, EXT_ROWS, 176):
        rows = slice(i, i + 176)
        s = sum(ext[k, rows, :].astype(F32) for k in range(4)) * 0.25
        ext[4, rows, :] = s.astype(BF16)

    def step(row, carry):
        qr = pl.ds(pl.multiple_of(row * STRIP, 32), STRIP)
        er = pl.ds(ext_row(row), LANES)
        for k in range(5):
            s = dot(q[k, qr, :], ext[k, er, :], NT) * SCALE
            s = pltpu.roll(s, 0, 1, stride=1, stride_axis=0)
            skew[k, qr, :] = s.astype(BF16)
        return carry

    lax.fori_loop(0, GRID, step, 0)

    def project(chunk, carry):
        rows = pl.ds(pl.multiple_of(chunk * 128, 128), 128)
        coarse[...] = dot(skew[4, rows, :], w_ref[1], NN)
        for k in range(4):
            flow_t[k, rows, :] = (dot(skew[k, rows, :], w_ref[0], NN) + coarse[...]).astype(BF16)
        return carry

    lax.fori_loop(0, 4, project, 0)
    acc = jnp.zeros((LANES, WIDTH), F32)
    for k in range(4):
        acc = acc + dot(skew[k], c[k], TN)
    acc2 = dot(skew[4], c[4], TN)
    for u in range(WINDOW):
        lo = u * PITCH + 12 + STRIP - 1
        proj[u * 9 : u * 9 + 9, :] = acc[lo : lo + 9]
        proj[81 + u * 9 : 81 + u * 9 + 9, :] = acc2[lo : lo + 9]
    join(perm[1], flow_t, flow, left_ref[0], None, 1)


def join(p, src, dst, left, mask, order=0):
    for half in range(2):
        slot = left if half == 0 else 1 - left
        for blk in range(4):
            v = jnp.concatenate(
                [src[k, strip_rows(blk, row, half ^ order), :] for k in range(4) for row in range(4)], axis=0
            )
            if mask is not None:
                v = v.astype(F32) * mask[slot].astype(F32)
            out = dot(v.astype(BF16), p, TN)
            dst[slot, :, blk * 256 : blk * 256 + 256] = out[: dst.shape[1]].astype(BF16)


def backward_kernel(perm, w_ref, q, ext, c, left_ref, mask,
                    g_first, centre, up, down, side, up_side, down_side, gext, gsc, gq):
    col = lax.axis_index("cols")
    gext[...] = jnp.zeros_like(gext)
    for k in range(5):
        gsc[k] = dot(c[k], w_ref[k // 4], NT) * SCALE

    def step(row, carry):
        qr = pl.ds(pl.multiple_of(row * STRIP, 32), STRIP)
        er = pl.ds(ext_row(row), LANES)
        terms = []
        for k in range(5):
            g = pltpu.roll(gsc[k, qr, :], 0, 1, stride=1, stride_axis=0).astype(BF16)
            terms.append(dot(g, ext[k, er, :], NN))
            gext[k, er, :] += dot(g, q[k, qr, :], TN)
        for k in range(4):
            gq[k, qr, :] = terms[k] + 0.25 * terms[4]
        return carry

    lax.fori_loop(0, GRID, step, 0)
    sub = lax.broadcasted_iota(jnp.int32, (16, WIDTH), 0)
    edge = jnp.where(col == 0, (sub < 4).astype(F32), (sub >= 12).astype(F32))
    for row in range(GRID + 2 * MARGIN):
        lo = 16 + row * PITCH
        er = pl.ds(ext_row(row + 1 - col), 16)
        coarse = 0.25 * gext[4, lo : lo + 32, :]
        coarse_side = 0.25 * gext[4, er, :]
        for k in range(4):
            v = gext[k, lo : lo + 32, :] + coarse
            s = ((gext[k, er, :] + coarse_side) * edge).astype(BF16)
            if row < MARGIN:
                up[k, row * 32 : row * 32 + 32, :] = v.astype(BF16)
                up_side[k, row * 16 : row * 16 + 16, :] = s
            elif row < GRID + MARGIN:
                at = row - MARGIN
                centre[k, at * 32 : at * 32 + 32, :] = v
                side[k, at * 16 : at * 16 + 16, :] = s
            else:
                at = row - GRID - MARGIN
                down[k, at * 32 : at * 32 + 32, :] = v.astype(BF16)
                down_side[k, at * 16 : at * 16 + 16, :] = s
    join(perm[0], gq, g_first, left_ref[0], mask)


def finish_kernel(perm, left_ref, mask, centre, above, below, side, above_side, below_side, g_second, total):
    col = lax.axis_index("cols")
    place = pl.multiple_of((1 - col) * 16, 16)
    total[...] = centre[...]
    for k in range(4):
        for row in range(GRID):
            rows = pl.ds(row * 32, 32)
            part = pl.ds(row * 32 + place, 16)
            sd = side[k, row * 16 : row * 16 + 16, :].astype(F32)
            if row < MARGIN:
                total[k, rows, :] += above[k, row * 32 : row * 32 + 32, :].astype(F32)
                sd = sd + above_side[k, row * 16 : row * 16 + 16, :].astype(F32)
            if row >= GRID - MARGIN:
                at = row - GRID + MARGIN
                total[k, rows, :] += below[k, at * 32 : at * 32 + 32, :].astype(F32)
                sd = sd + below_side[k, at * 16 : at * 16 + 16, :].astype(F32)
            total[k, part, :] += sd
    join(perm[0], total, g_second, left_ref[0], mask)


def vm():
    return pl.BlockSpec(memory_space=pltpu.VMEM)


def sm():
    return pl.BlockSpec(memory_space=pltpu.SMEM)


def sds(shape, dtype):
    return jax.ShapeDtypeStruct(shape, dtype)


PARAMS = pltpu.CompilerParams(vmem_limit_bytes=48 * 1024 * 1024)


def shards(earlier, later, cot, weight, owner, labels, mask):
    rows = lax.axis_size("rows")
    cols = lax.axis_size("cols")
    base = (lax.axis_index("rows") * cols + lax.axis_index("cols")) * 2
    right_of = labels[0, 3]
    left_of = labels[1, 2]
    is_first = ((right_of >= 0) & (owner[jnp.maximum(right_of, 0)] == base + 1)) | (
        (left_of >= 0) & (owner[jnp.maximum(left_of, 0)] == base)
    )
    left = jnp.where(is_first, 0, 1).astype(jnp.int32)[None]
    perm = jnp.stack([permutation(False), permutation(True)])
    wide = jnp.pad(weight.reshape(2, 9, 9, WIDTH), ((0, 0), (0, 0), (0, PITCH - 9), (0, 0)))
    wide = wide.reshape(2, 9 * PITCH, WIDTH)
    wide, wide_back = (
        jnp.pad(wide, ((0, 0), (lo, LANES - 9 * PITCH - lo), (0, 0))) for lo in (12, 12 + STRIP - 1)
    )

    pos = GRID * STRIP
    q, e, c, q_back, c_back, side, upc, downc = pl.pallas_call(
        split_kernel,
        out_shape=(
            sds((5, pos, WIDTH), BF16),
            sds((4, pos, WIDTH), BF16),
            sds((5, pos, WIDTH), BF16),
            sds((5, pos, WIDTH), BF16),
            sds((5, pos, WIDTH), BF16),
            sds((4, GRID * 16, WIDTH), BF16),
            sds((4, MARGIN * 16, WIDTH), BF16),
            sds((4, MARGIN * 16, WIDTH), BF16),
        ),
        in_specs=[sm(), sm(), sm(), vm(), vm(), vm(), vm()],
        out_specs=(vm(),) * 8,
        compiler_params=PARAMS,
    )(owner, labels, mask, perm, earlier, later, cot)

    up_pairs = [(i + 1, i) for i in range(rows - 1)]
    down_pairs = [(i, i + 1) for i in range(rows - 1)]
    cross = [(0, 1), (1, 0)]

    def diagonal(pairs):
        return [(a * cols + x, b * cols + y) for a, b in pairs for x, y in cross]

    def exchange(up, down, side, up_side, down_side):
        return (
            lax.ppermute(down, "rows", down_pairs),
            lax.ppermute(up, "rows", up_pairs),
            lax.ppermute(side, "cols", cross),
            lax.ppermute(down_side, ("rows", "cols"), diagonal(down_pairs)),
            lax.ppermute(up_side, ("rows", "cols"), diagonal(up_pairs)),
        )

    halo = exchange(e[:, : MARGIN * STRIP], e[:, pos - MARGIN * STRIP :], side, upc, downc)
    ext, flow, proj = pl.pallas_call(
        forward_kernel,
        out_shape=(
            sds((5, EXT_ROWS, WIDTH), BF16),
            sds((2, WIDTH, 1024), BF16),
            sds((162, WIDTH), F32),
        ),
        in_specs=[vm()] * 10 + [sm()],
        out_specs=(vm(),) * 3,
        scratch_shapes=[pltpu.VMEM((5, pos, LANES), BF16), pltpu.VMEM((4, pos, WIDTH), BF16), pltpu.VMEM((128, WIDTH), F32)],
        compiler_params=PARAMS,
    )(perm, wide_back, q_back, e, *halo, c_back, left)
    proj = lax.psum(proj, ("rows", "cols")) * (1.0 / math.sqrt(2 * rows * cols * 1024))
    rim = (4, MARGIN * STRIP, WIDTH)
    corner = (4, MARGIN * 16, WIDTH)
    g_first, centre, *rims = pl.pallas_call(
        backward_kernel,
        out_shape=(
            sds((2, CHANNELS, 1024), BF16),
            sds((4, pos, WIDTH), F32),
            sds(rim, BF16),
            sds(rim, BF16),
            sds((4, GRID * 16, WIDTH), BF16),
            sds(corner, BF16),
            sds(corner, BF16),
        ),
        in_specs=[vm()] * 5 + [sm()] * 2,
        out_specs=(vm(),) * 7,
        scratch_shapes=[
            pltpu.VMEM((5, EXT_ROWS, WIDTH), F32),
            pltpu.VMEM((5, pos, LANES), F32),
            pltpu.VMEM((4, pos, WIDTH), F32),
        ],
        compiler_params=PARAMS,
    )(perm, wide, q, ext, c, left, mask)
    got_above, got_below, got_side, got_above_side, got_below_side = exchange(*rims)
    g_second = pl.pallas_call(
        finish_kernel,
        out_shape=sds((2, CHANNELS, 1024), BF16),
        in_specs=[vm(), sm(), sm()] + [vm()] * 6,
        out_specs=vm(),
        scratch_shapes=[pltpu.VMEM((4, pos, WIDTH), F32)],
        compiler_params=PARAMS,
    )(perm, left, mask, centre, got_above, got_below, got_side, got_above_side, got_below_side)
    return flow, g_first, g_second, proj


def solution(mesh):
    spec = P(("groups", "rows", "cols"), None, None)
    return jax.shard_map(
        shards,
        mesh=mesh,
        in_specs=(spec, spec, spec, P(), P("groups"), P(("groups", "rows", "cols"), None), P(("groups", "rows", "cols"))),
        out_specs=(spec, spec, spec, P("groups", None)),
        check_vma=False,
    )
```

profile of v0, /device:TPU:1, one launch (start us, length us, event | category | flops | bytes accessed | tf_op | source)
XLA Modules:
  0.0 151.2 jit_solution(1266165929805917120)
XLA Ops:
  7.2 0.0 copy-start.17
  7.2 0.0 copy-start.21
  7.2 0.0 all-reduce.5.cloned.1.call-start
  7.3 0.1 select_convert_fusion
  7.4 0.0 copy-start.8
  7.4 1.0 copy-done.8
  8.5 0.0 copy-start.9
  8.5 1.0 copy-done.9
  9.5 1.0 copy-done.10
  10.5 0.7 copy-done.16
  11.1 0.7 copy-done.18
  11.8 0.7 copy-done.20
  12.5 2.9 %shard_map.102 = (bf16[5,512,128]{2,1,0:T(8,128)(2,1)S(1)}, bf16[4,512,128]{2,1,0:T(8,128)(2,1)S(1)}, bf16[5,512,128]{2,1,0:T(8,128)(2,1)S(1)}, bf16[5,512,128]{...) custom-call(s32[32]{0:T(128)S(1)} %copy-done.16, ...), custom_call_target="tpu_custom_call" | custom-call | tf_op jit(solution)/shard_map/pallas_call | solution.py:264
  15.3 0.9 copy-done.6
  16.2 5.1 %collective-permute-start.3 = (bf16[4,64,128]{2,1,0:T(8,128)(2,1)}, bf16[4,64,128]{2,1,0:T(8,128)(2,1)}, u32[]{:S(2)}, u32[]{:S(2)}) collective-permute-start(bf16[4,64,128]{2,1,0:T(8,128)(2,1)} %get-tuple-element.25), channel_id=1, source_target_pairs={{0,3},{1,2},{2,5},{3,4},{4,7},{5,6},{6,9},{7,8},{8,11},{9,10},{10,... | collective-permute-start | bytes 196616 | tf_op jit(solution)/shard_map/ppermute | solution.py:293
  21.3 1.3 collective-permute-start.4
  22.6 0.1 collective-permute-start.2
  22.7 0.7 fusion.12
  23.4 1.3 collective-permute-start.1
  24.7 5.0 %collective-permute-start = (bf16[4,128,128]{2,1,0:T(8,128)(2,1)}, bf16[4,128,128]{2,1,0:T(8,128)(2,1)S(1)}, u32[]{:S(2)}, u32[]{:S(2)}) collective-permute-start(bf16[4,128,128]{2,1,0:T(8,128)(2,1)} %get-tuple-element.41), channel_id=1, source_target_pairs={{0,2},{2,4},{4,6},{6,8},{8,10},{10,12},{12,14},{1,3},{3,5},{5,7},{... | collective-permute-start | bytes 393224 | tf_op jit(solution)/shard_map/ppermute | solution.py:290
  29.7 0.7 fusion.14
  33.0 0.0 copy-done.17
  33.0 0.7 fusion.15
  34.3 0.0 copy-done.21
  35.1 0.1 fusion.13
  35.2 0.0 copy-start.19
  35.2 0.0 collective-permute-done.3.above_side
  35.2 0.0 collective-permute-done.4.below_side
  35.2 0.0 collective-permute-done.1.below
  35.2 0.0 copy-start.11
  35.2 0.6 copy-done.11
  35.9 0.0 collective-permute-done.above
  35.9 0.7 copy-done.13
  36.5 0.0 collective-permute-done.2.side
  36.5 0.0 copy-done.2
  36.5 0.0 copy-done.4
  36.5 0.0 copy-start.5
  36.5 1.1 copy-done.5
  37.6 1.1 copy-done.7
  38.7 0.9 copy-done.12
  39.6 0.9 copy-done.14
  40.5 10.8 %shard_map.103 = (bf16[5,1232,128]{2,1,0:T(8,128)(2,1)S(1)}, bf16[2,128,1024]{2,1,0:T(8,128)(2,1)}, f32[162,128]{1,0:T(8,128)S(1)}) custom-call(bf16[2,256,256]{2,1,0:T(8,128)(2,1)S(1)} %pad_maximum_fusion.perm, bf16[2,512,128]{2,1,0:T(8,128)(2,1)S(1)} %get-tuple-element.43.w_ref, bf16[5,512,128]{2,1,0:T(8,128)(2,1)S(1)} %copy-done.5, ...), custom_call_target="tpu_custom_call" | custom-call | tf_op jit(solution)/shard_map/pallas_call | solution.py:298
  51.4 0.6 copy-done.15
  52.0 0.0 all-reduce.5.cloned.1.call-update
  52.0 0.0 copy-done.19
  52.0 0.0 copy-start.3
  52.0 1.1 copy-done.3
  53.1 13.1 %shard_map.104 = (bf16[2,96,1024]{2,1,0:T(8,128)(2,1)}, f32[4,512,128]{2,1,0:T(8,128)S(1)}, bf16[4,128,128]{2,1,0:T(8,128)(2,1)S(1)}, bf16[4,128,128]{2,1,0:T(8,...) custom-call(bf16[2,256,256]{2,1,0:T(8,128)(2,1)S(1)} %pad_maximum_fu, ...), custom_call_target="tpu_custom_call" | custom-call | tf_op jit(solution)/shard_map/pallas_call | solution.py:313
  66.3 1.0 copy-done
  67.2 0.3 collective-permute-start.7
  67.5 4.4 %collective-permute-start.8 = (bf16[4,64,128]{2,1,0:T(8,128)(2,1)S(1)}, bf16[4,64,128]{2,1,0:T(8,128)(2,1)S(1)}, u32[]{:S(2)}, u32[]{:S(2)}) collective-permute-start(bf16[4,64,128]{2,1,0:T(8,128)(2,1)S(1)} %get-tuple-element.37), channel_id=1, source_target_pairs={{0,3},{1,2},{2,5},{3,4},{4,7},{5,6},{6,9},{7,8},{8,11},{9,10},{10,... | collective-permute-start | bytes 196616 | tf_op jit(solution)/shard_map/ppermute | solution.py:293
  71.9 1.3 collective-permute-start.9
  73.2 4.4 %collective-permute-start.5 = (bf16[4,128,128]{2,1,0:T(8,128)(2,1)S(1)}, bf16[4,128,128]{2,1,0:T(8,128)(2,1)S(1)}, u32[]{:S(2)}, u32[]{:S(2)}) collective-permute-start(bf16[4,128,128]{2,1,0:T(8,128)(2,1)S(1)} %get-tuple-element.34), channel_id=1, source_target_pairs={{0,2},{2,4},{4,6},{6,8},{8,10},{10,12},{12,14},{1,3},{3,5},{5,7},{... | collective-permute-start | bytes 393224 | tf_op jit(solution)/shard_map/ppermute | solution.py:290
  77.6 1.3 collective-permute-start.6
  78.9 60.5 %all-reduce.5.cloned.1.call-done = f32[162,128]{1,0:T(8,128)} async-done(((f32[162,128]{1,0:T(8,128)}), f32[162,128]{1,0:T(8,128)}) %all-reduce.5.cloned.1.call-update) | async-done | bytes 82960 | tf_op jit(solution)/shard_map/psum | solution.py:310
  139.4 1.5 %broadcast_multiply_fusion = f32[162,128]{1,0:T(8,128)} fusion(f32[162,128]{1,0:T(8,128)} %all-reduce.5.cloned.1.call-done), kind=kLoop, calls=%fused_computation.5 | loop fusion | flops 20736 | bytes 165888 | tf_op jit(solution)/shard_map/mul | solution.py:310
  141.0 0.0 collective-permute-done.8.above_side
  141.0 0.0 collective-permute-done.9.below_side
  141.0 0.0 collective-permute-done.5.above
  141.0 0.0 collective-permute-done.6.below
  141.0 0.0 collective-permute-done.7.side
  141.0 0.0 copy-start.1
  141.0 1.2 copy-done.1
  142.2 2.1 %shard_map.105 = bf16[2,96,1024]{2,1,0:T(8,128)(2,1)} custom-call(bf16[2,256,256]{2,1,0:T(8,128)(2,1)S(1)} %pad_maximum_fusion.perm, s32[1]{0:T(128)} %bitcast.7.left_ref, s32[2]{0:T(128)S(1)} %copy-done.19, f32[4,512,128]{2,1,0:T(8,128)S(1)} %copy-done.1, bf16[4,128,128]{2,1,0:T(8,128)(2,1)S(1)} %collective-permute-done.5.above, ...), custom_call_target="tpu_custom_call" | custom-call | tf_op jit(solution)/shard_map/pallas_call | solution.py:334
  (18 shorter events, 0.1 us)
Async XLA Ops:
  7.2 25.8 %copy-start.17 = (s32[32]{0:T(128)S(1)}, s32[32]{0:T(128)}, u32[]{:S(2)}) copy-start(s32[32]{0:T(128)} %owner.1) | copy-start | bytes 388
  7.2 27.2 %copy-start.21 = (bf16[162,128]{1,0:T(8,128)(2,1)S(1)}, bf16[162,128]{1,0:T(8,128)(2,1)}, u32[]{:S(2)}) copy-start(bf16[162,128]{1,0:T(8,128)(2,1)} %param.10) | copy-start | bytes 124420
  7.2 132.3 %all-reduce.5.cloned.1.call-start = ((), (), s32[]{:S(2)}) async-start(), calls=%async_computation | async-start | bytes 172032 | tf_op jit(solution)/shard_map/psum | solution.py:310
  7.4 1.0 copy-start.8
  8.5 1.0 copy-start.9
  9.5 1.0 copy-start.10
  10.5 0.7 copy-start.16
  11.1 0.7 copy-start.18
  11.8 0.7 copy-start.20
  15.3 0.9 copy-start.6
  16.2 20.3 %copy-start.2 = (bf16[5,512,128]{2,1,0:T(8,128)(2,1)}, bf16[5,512,128]{2,1,0:T(8,128)(2,1)S(1)}, u32[]{:S(2)}) copy-start(bf16[5,512,128]{2,1,0:T(8,128)(2,1)S(1)} %get-tuple-element.31.c) | copy-start | bytes 1966084
  16.2 20.3 %copy-start.4 = (bf16[5,512,128]{2,1,0:T(8,128)(2,1)}, bf16[5,512,128]{2,1,0:T(8,128)(2,1)S(1)}, u32[]{:S(2)}) copy-start(bf16[5,512,128]{2,1,0:T(8,128)(2,1)S(1)} %get-tuple-element.22.q) | copy-start | bytes 1966084
  16.2 19.0 %collective-permute-start.3 = (bf16[4,64,128]{2,1,0:T(8,128)(2,1)}, bf16[4,64,128]{2,1,0:T(8,128)(2,1)}, u32[]{:S(2)}, u32[]{:S(2)}) collective-permute-start(bf16[4,64,128]{2,1,0:T(8,128)(2,1)} %get-tuple-element.25), channel_id=1, source_target_pairs={{0,3},{1,2},{2,5},{3,4},{4,7},{5,6},{6,9},{7,8},{8,11},{9,10},{10,... | collective-permute-start | bytes 196616 | tf_op jit(solution)/shard_map/ppermute | solution.py:293
  21.3 13.9 %collective-permute-start.4 = (bf16[4,64,128]{2,1,0:T(8,128)(2,1)}, bf16[4,64,128]{2,1,0:T(8,128)(2,1)}, u32[]{:S(2)}, u32[]{:S(2)}) collective-permute-start(bf16[4,64,128]{2,1,0:T(8,128)(2,1)} %get-tuple-element.26), channel_id=1, source_target_pairs={{2,1},{3,0},{4,3},{5,2},{6,5},{7,4},{8,7},{9,6},{10,9},{11,8},{12,... | collective-permute-start | bytes 196616 | tf_op jit(solution)/shard_map/ppermute | solution.py:294
  22.6 13.9 %collective-permute-start.2 = (bf16[4,256,128]{2,1,0:T(8,128)(2,1)}, bf16[4,256,128]{2,1,0:T(8,128)(2,1)S(1)}, u32[]{:S(2)}, u32[]{:S(2)}) collective-permute-start(bf16[4,256,128]{2,1,0:T(8,128)(2,1)} %get-tuple-element.24), channel_id=1, source_target_pairs={{0,1},{1,0},{2,3},{3,2},{4,5},{5,4},{6,7},{7,6},{8,9},{9,8},{10,11... | collective-permute-start | bytes 786440 | tf_op jit(solution)/shard_map/ppermute | solution.py:292
  23.4 11.8 %collective-permute-start.1 = (bf16[4,128,128]{2,1,0:T(8,128)(2,1)}, bf16[4,128,128]{2,1,0:T(8,128)(2,1)S(1)}, u32[]{:S(2)}, u32[]{:S(2)}) collective-permute-start(bf16[4,128,128]{2,1,0:T(8,128)(2,1)} %get-tuple-element.40), channel_id=1, source_target_pairs={{2,0},{4,2},{6,4},{8,6},{10,8},{12,10},{14,12},{3,1},{5,3},{7,5},{... | collective-permute-start | bytes 393224 | tf_op jit(solution)/shard_map/ppermute | solution.py:291
  24.7 11.2 %collective-permute-start = (bf16[4,128,128]{2,1,0:T(8,128)(2,1)}, bf16[4,128,128]{2,1,0:T(8,128)(2,1)S(1)}, u32[]{:S(2)}, u32[]{:S(2)}) collective-permute-start(bf16[4,128,128]{2,1,0:T(8,128)(2,1)} %get-tuple-element.41), channel_id=1, source_target_pairs={{0,2},{2,4},{4,6},{6,8},{8,10},{10,12},{12,14},{1,3},{3,5},{5,7},{... | collective-permute-start | bytes 393224 | tf_op jit(solution)/shard_map/ppermute | solution.py:290
  35.2 16.8 %copy-start.19 = (s32[2]{0:T(128)S(1)}, s32[2]{0:T(128)}, u32[]{:S(2)}) copy-start(s32[2]{0:T(128)} %mask.5) | copy-start | bytes 28
  35.2 0.6 copy-start.11
  35.9 0.7 copy-start.13
  36.5 1.1 copy-start.5
  37.6 1.1 copy-start.7
  38.7 0.9 copy-start.12
  39.6 0.9 copy-start.14
  51.3 0.6 copy-start.15
  52.0 1.1 copy-start.3
  66.2 1.0 copy-start
  67.2 73.8 %collective-permute-start.7 = (bf16[4,256,128]{2,1,0:T(8,128)(2,1)S(1)}, bf16[4,256,128]{2,1,0:T(8,128)(2,1)S(1)}, u32[]{:S(2)}, u32[]{:S(2)}) collective-permute-start(bf16[4,256,128]{2,1,0:T(8,128)(2,1)S(1)} %get-tuple-element.36), channel_id=1, source_target_pairs={{0,1},{1,0},{2,3},{3,2},{4,5},{5,4},{6,7},{7,6},{8,9},{9,8},{10,11... | collective-permute-start | bytes 786440 | tf_op jit(solution)/shard_map/ppermute | solution.py:292
  67.5 73.5 %collective-permute-start.8 = (bf16[4,64,128]{2,1,0:T(8,128)(2,1)S(1)}, bf16[4,64,128]{2,1,0:T(8,128)(2,1)S(1)}, u32[]{:S(2)}, u32[]{:S(2)}) collective-permute-start(bf16[4,64,128]{2,1,0:T(8,128)(2,1)S(1)} %get-tuple-element.37), channel_id=1, source_target_pairs={{0,3},{1,2},{2,5},{3,4},{4,7},{5,6},{6,9},{7,8},{8,11},{9,10},{10,... | collective-permute-start | bytes 196616 | tf_op jit(solution)/shard_map/ppermute | solution.py:293
  71.9 69.1 %collective-permute-start.9 = (bf16[4,64,128]{2,1,0:T(8,128)(2,1)S(1)}, bf16[4,64,128]{2,1,0:T(8,128)(2,1)S(1)}, u32[]{:S(2)}, u32[]{:S(2)}) collective-permute-start(bf16[4,64,128]{2,1,0:T(8,128)(2,1)S(1)} %get-tuple-element.38), channel_id=1, source_target_pairs={{2,1},{3,0},{4,3},{5,2},{6,5},{7,4},{8,7},{9,6},{10,9},{11,8},{12,... | collective-permute-start | bytes 196616 | tf_op jit(solution)/shard_map/ppermute | solution.py:294
  73.2 67.8 %collective-permute-start.5 = (bf16[4,128,128]{2,1,0:T(8,128)(2,1)S(1)}, bf16[4,128,128]{2,1,0:T(8,128)(2,1)S(1)}, u32[]{:S(2)}, u32[]{:S(2)}) collective-permute-start(bf16[4,128,128]{2,1,0:T(8,128)(2,1)S(1)} %get-tuple-element.34), channel_id=1, source_target_pairs={{0,2},{2,4},{4,6},{6,8},{8,10},{10,12},{12,14},{1,3},{3,5},{5,7},{... | collective-permute-start | bytes 393224 | tf_op jit(solution)/shard_map/ppermute | solution.py:290
  77.6 63.4 %collective-permute-start.6 = (bf16[4,128,128]{2,1,0:T(8,128)(2,1)S(1)}, bf16[4,128,128]{2,1,0:T(8,128)(2,1)S(1)}, u32[]{:S(2)}, u32[]{:S(2)}) collective-permute-start(bf16[4,128,128]{2,1,0:T(8,128)(2,1)S(1)} %get-tuple-element.35), channel_id=1, source_target_pairs={{2,0},{4,2},{6,4},{8,6},{10,8},{12,10},{14,12},{3,1},{5,3},{7,5},{... | collective-permute-start | bytes 393224 | tf_op jit(solution)/shard_map/ppermute | solution.py:291
  141.0 1.2 copy-start.1
Sparse Core Ops, SparseCore 0:
  52.1 87.2 all-reduce.4
where the time goes:
time: 152 us; the launch traced here: 151 us
  waiting for transfers between devices  60.6 us (40%)
  Pallas kernels  29 us (19%)
  starting transfers between devices  24.5 us (16%)
  between operations  18.2 us (12%)
  local copies, waits for them, and re-layouts  17.3 us (11%)
  other arithmetic  1.71 us (1%)
    psum x1, waiting for transfers between devices, shards(): lax.psum(proj, ('rows', 'cols')) * (1.0 / math.sqrt(2 * rows * cols * 1024))  60.5 us
    unnamed x44, local copies, waits for them, and re-layouts  15.1 us
    pallas_call x1, Pallas kernels, shards(): pl.pallas_call(backward_kernel, out_shape=(sds((2, CHANNELS, 1024), BF16)...  13.1 us
    pallas_call x1, Pallas kernels, shards(): pl.pallas_call(forward_kernel, out_shape=(sds((5, EXT_ROWS, WIDTH), BF16)...  10.8 us
    ppermute x2, starting transfers between devices, exchange(): lax.ppermute(down_side, ('rows', 'cols'), diagonal(down_pairs))  9.54 us
    ppermute x2, starting transfers between devices, exchange(): lax.ppermute(down, 'rows', down_pairs)  9.39 us
  transfers between devices with their start and end apart: 11, of which 1 were waited for; matrix products, arithmetic and copies ran while one was open for 2% of the time, Pallas kernels for 9%

commit v1 on v0

--- a/solution.py
+++ b/solution.py
@@ -307,7 +307,12 @@
         scratch_shapes=[pltpu.VMEM((5, pos, LANES), BF16), pltpu.VMEM((4, pos, WIDTH), BF16), pltpu.VMEM((128, WIDTH), F32)],
         compiler_params=PARAMS,
     )(perm, wide_back, q_back, e, *halo, c_back, left)
-    proj = lax.psum(proj, ("rows", "cols")) * (1.0 / math.sqrt(2 * rows * cols * 1024))
+    proj = proj + lax.ppermute(proj, "cols", cross)
+    distance = 1
+    while distance < rows:
+        proj = proj + lax.ppermute(proj, "rows", [(i, i ^ distance) for i in range(rows)])
+        distance *= 2
+    proj = proj * (1.0 / math.sqrt(2 * rows * cols * 1024))
     rim = (4, MARGIN * STRIP, WIDTH)
     corner = (4, MARGIN * 16, WIDTH)
     g_first, centre, *rims = pl.pallas_call(

time: 152 us -> 82.6 us (0.54)
  waiting for transfers between devices: 60.6 us -> 7.49 us
  between operations: 18.2 us -> 4.65 us
  local copies, waits for them, and re-layouts: 17.3 us -> 9.49 us
  starting transfers between devices: 24.5 us -> 29.8 us
    psum x1 -> x0, waiting for transfers between devices: 60.5 us -> none  [shards(): lax.psum(proj, ('rows', 'cols')) * (1.0 / math.sqrt(2 * rows * cols * 1024))]
    unnamed x44 -> x16, local copies, waits for them, and re-layouts: 15.1 us -> 5.03 us
    ppermute x0 -> x4, starting transfers between devices: none -> 6.36 us  [the longest x3 6.06 us: shards(): lax.ppermute(proj, 'rows', [(i, i ^ distance) for i in range(rows)])]
    ppermute x2, waiting for transfers between devices: 0.01 us -> 5.02 us  [exchange(): lax.ppermute(up_side, ('rows', 'cols'), diagonal(up_pairs))]
    ppermute x0 -> x4, waiting for transfers between devices: none -> 2.45 us  [the longest x3 2.45 us: shards(): lax.ppermute(proj, 'rows', [(i, i ^ distance) for i in range(rows)])]
  transfers between devices with their start and end apart: 11 -> 14, of which waited for: 1 -> 2; matrix products, arithmetic and copies ran while one was open for 2% -> 6% of each run, Pallas kernels for 9% -> 19%
where the time goes in v1:
time: 82.6 us; the launch traced here: 81.5 us
  starting transfers between devices  29.8 us (36%)
  Pallas kernels  29.2 us (35%)
  local copies, waits for them, and re-layouts  9.49 us (11%)
  waiting for transfers between devices  7.49 us (9%)
  between operations  4.65 us (6%)
  other arithmetic  0.87 us (1%)
    pallas_call x1, Pallas kernels, shards(): pl.pallas_call(backward_kernel, out_shape=(sds((2, CHANNELS, 1024), BF16)...  13.2 us
    pallas_call x1, Pallas kernels, shards(): pl.pallas_call(forward_kernel, out_shape=(sds((5, EXT_ROWS, WIDTH), BF16)...  11 us
    ppermute x2, starting transfers between devices, exchange(): lax.ppermute(down_side, ('rows', 'cols'), diagonal(down_pairs))  10 us
    ppermute x2, starting transfers between devices, exchange(): lax.ppermute(down, 'rows', down_pairs)  8 us
    ppermute x3, starting transfers between devices, shards(): lax.ppermute(proj, 'rows', [(i, i ^ distance) for i in range(rows)])  6.06 us
    unnamed x16, local copies, waits for them, and re-layouts  5.03 us
    ppermute x2, waiting for transfers between devices, exchange(): lax.ppermute(up_side, ('rows', 'cols'), diagonal(up_pairs))  5.02 us
    pallas_call x1, Pallas kernels, shards(): pl.pallas_call(split_kernel, out_shape=(sds((5, pos, WIDTH), BF16), sds((...  2.89 us
  transfers between devices with their start and end apart: 14, of which 2 were waited for; matrix products, arithmetic and copies ran while one was open for 6% of the time, Pallas kernels for 19%

profile of v1, /device:TPU:1, one launch (start us, length us, event | category | flops | bytes accessed | tf_op | source)
XLA Modules:
  0.0 81.5 jit_solution(16430396400363504903)
XLA Ops:
  0.6 0.0 copy-start.4
  0.7 0.1 select_convert_fusion
  0.8 0.0 copy-start
  0.9 1.0 %copy-done = bf16[2,128,1024]{2,1,0:T(8,128)(2,1)S(1)} copy-done((bf16[2,128,1024]{2,1,0:T(8,128)(2,1)S(1)}, bf16[2,128,1024]{2,1,0:T(8,128)(2,1)}, u32[]{:S(2)}) %copy-start) | copy-done | bytes 524312
  1.9 0.0 copy-start.1
  1.9 1.0 %copy-done.1 = bf16[2,96,1024]{2,1,0:T(8,128)(2,1)S(1)} copy-done((bf16[2,96,1024]{2,1,0:T(8,128)(2,1)S(1)}, bf16[2,96,1024]{2,1,0:T(8,128)(2,1)}, u32[]{:S(2)}) %copy-start.1) | copy-done | bytes 393240
  2.9 0.0 copy-start.2
  2.9 1.0 %copy-done.2 = bf16[2,96,1024]{2,1,0:T(8,128)(2,1)S(1)} copy-done((bf16[2,96,1024]{2,1,0:T(8,128)(2,1)S(1)}, bf16[2,96,1024]{2,1,0:T(8,128)(2,1)}, u32[]{:S(2)}) %copy-start.2) | copy-done | bytes 393240
  3.9 0.0 copy-start.3
  3.9 0.7 copy-done.3
  4.5 0.0 copy-start.5
  4.5 0.7 copy-done.5
  5.2 0.0 copy-start.7
  5.2 0.7 copy-done.7
  5.9 2.9 %shard_map.102 = (bf16[5,512,128]{2,1,0:T(8,128)(2,1)S(1)}, bf16[4,512,128]{2,1,0:T(8,128)(2,1)S(1)}, bf16[5,512,128]{2,1,0:T(8,128)(2,1)S(1)}, bf16[5,512,128]{...) custom-call(s32[32]{0:T(128)S(1)} %copy-done.3, ...), custom_call_target="tpu_custom_call" | custom-call | tf_op jit(solution)/shard_map/pallas_call | solution.py:264
  8.8 5.1 %collective-permute-start.3 = (bf16[4,64,128]{2,1,0:T(8,128)(2,1)}, bf16[4,64,128]{2,1,0:T(8,128)(2,1)}, u32[]{:S(2)}, u32[]{:S(2)}) collective-permute-start(bf16[4,64,128]{2,1,0:T(8,128)(2,1)} %get-tuple-element.25), channel_id=1, source_target_pairs={{0,3},{1,2},{2,5},{3,4},{4,7},{5,6},{6,9},{7,8},{8,11},{9,10},{10,... | collective-permute-start | bytes 196616 | tf_op jit(solution)/shard_map/ppermute | solution.py:293
  13.9 1.3 %collective-permute-start.4 = (bf16[4,64,128]{2,1,0:T(8,128)(2,1)}, bf16[4,64,128]{2,1,0:T(8,128)(2,1)}, u32[]{:S(2)}, u32[]{:S(2)}) collective-permute-start(bf16[4,64,128]{2,1,0:T(8,128)(2,1)} %get-tuple-element.26), channel_id=1, source_target_pairs={{2,1},{3,0},{4,3},{5,2},{6,5},{7,4},{8,7},{9,6},{10,9},{11,8},{12,... | collective-permute-start | bytes 196616 | tf_op jit(solution)/shard_map/ppermute | solution.py:294
  15.2 0.1 collective-permute-start.2
  15.2 0.7 fusion.12
  16.0 1.3 %collective-permute-start.1 = (bf16[4,128,128]{2,1,0:T(8,128)(2,1)}, bf16[4,128,128]{2,1,0:T(8,128)(2,1)S(1)}, u32[]{:S(2)}, u32[]{:S(2)}) collective-permute-start(bf16[4,128,128]{2,1,0:T(8,128)(2,1)} %get-tuple-element.40), channel_id=1, source_target_pairs={{2,0},{4,2},{6,4},{8,6},{10,8},{12,10},{14,12},{3,1},{5,3},{7,5},{... | collective-permute-start | bytes 393224 | tf_op jit(solution)/shard_map/ppermute | solution.py:291
  17.3 5.6 %collective-permute-start = (bf16[4,128,128]{2,1,0:T(8,128)(2,1)}, bf16[4,128,128]{2,1,0:T(8,128)(2,1)}, u32[]{:S(2)}, u32[]{:S(2)}) collective-permute-start(bf16[4,128,128]{2,1,0:T(8,128)(2,1)} %get-tuple-element.41), channel_id=1, source_target_pairs={{0,2},{2,4},{4,6},{6,8},{8,10},{10,12},{12,14},{1,3},{3,5},{5,7},{... | collective-permute-start | bytes 393224 | tf_op jit(solution)/shard_map/ppermute | solution.py:290
  22.9 0.6 fusion.14
  26.1 0.0 copy-done.4
  26.1 0.6 fusion.15
  27.4 1.4 %reshape.96 = bf16[2,9,9,128]{3,2,1,0:T(8,128)(2,1)} reshape(bf16[162,128]{1,0:T(8,128)(2,1)} %param.10) | data formatting | bytes 82944 | tf_op jit(solution)/shard_map/reshape | solution.py:257
  29.4 0.9 %pad.12 = bf16[2,9,48,128]{3,2,1,0:T(8,128)(2,1)S(1)} pad(bf16[2,9,9,128]{3,2,1,0:T(8,128)(2,1)} %reshape.96, bf16[]{:T(256)} %constant.38.clone.1), padding=0_0x0_0x0_39x0_0 | pad | bytes 262658 | tf_op jit(solution)/shard_map/jit(_pad)/pad | solution.py:257
  30.4 0.1 fusion.13
  30.5 0.0 copy-start.6
  30.5 0.0 collective-permute-done.3.above_side
  30.5 0.0 collective-permute-done.4.below_side
  30.5 0.0 collective-permute-done.1.below
  30.5 0.0 collective-permute-done.above
  30.5 0.0 collective-permute-done.2.side
  30.5 11.0 %shard_map.103 = (bf16[5,1232,128]{2,1,0:T(8,128)(2,1)S(1)}, bf16[2,128,1024]{2,1,0:T(8,128)(2,1)}, f32[162,128]{1,0:T(8,128)S(1)}) custom-call(bf16[2,256,256]{2,1,0:T(8,128)(2,1)S(1)} %pad_maximum_fusion.perm, bf16[2,512,128]{2,1,0:T(8,128)(2,1)S(1)} %get-tuple-element.43.w_ref, bf16[5,512,128]{2,1,0:T(8,128)(2,1)S(1)} %get-tuple-element.22.q, ...), custom_call_target="tpu_custom_call" | custom-call | tf_op jit(solution)/shard_map/pallas_call | solution.py:298
  41.5 0.3 collective-permute-start.10
  41.8 0.0 copy-done.6
  41.8 13.2 %shard_map.104 = (bf16[2,96,1024]{2,1,0:T(8,128)(2,1)}, f32[4,512,128]{2,1,0:T(8,128)S(1)}, bf16[4,128,128]{2,1,0:T(8,128)(2,1)S(1)}, bf16[4,128,128]{2,1,0:T(8,...) custom-call(bf16[2,256,256]{2,1,0:T(8,128)(2,1)S(1)} %pad_maximum_fu, ...), custom_call_target="tpu_custom_call" | custom-call | tf_op jit(solution)/shard_map/pallas_call | solution.py:318
  55.0 0.2 collective-permute-start.7
  55.2 0.0 collective-permute-done.10
  55.2 1.9 %collective-permute-start.11 = (f32[162,128]{1,0:T(8,128)S(1)}, f32[162,128]{1,0:T(8,128)S(1)}, u32[]{:S(2)}, u32[]{:S(2)}) collective-permute-start(f32[162,128]{1,0:T(8,128)S(1)} %add.61), channel_id=1, source_target_pairs={{0,2},{2,0},{4,6},{6,4},{8,10},{10,8},{12,14},{14,12},{1,3},{3,1},... | collective-permute-start | bytes 248840 | tf_op jit(solution)/shard_map/ppermute | solution.py:313
  57.1 2.4 %collective-permute-done.11 = f32[162,128]{1,0:T(8,128)S(1)} collective-permute-done((f32[162,128]{1,0:T(8,128)S(1)}, f32[162,128]{1,0:T(8,128)S(1)}, u32[]{:S(2)}, u32[]{:S(2)}) %collective-permute-start.11) | collective-permute-done | bytes 82976 | tf_op jit(solution)/shard_map/ppermute | solution.py:313
  59.6 0.5 collective-permute-start.12
  60.0 4.9 %collective-permute-start.8 = (bf16[4,64,128]{2,1,0:T(8,128)(2,1)S(1)}, bf16[4,64,128]{2,1,0:T(8,128)(2,1)S(1)}, u32[]{:S(2)}, u32[]{:S(2)}) collective-permute-start(bf16[4,64,128]{2,1,0:T(8,128)(2,1)S(1)} %get-tuple-element.37), channel_id=1, source_target_pairs={{0,3},{1,2},{2,5},{3,4},{4,7},{5,6},{6,9},{7,8},{8,11},{9,10},{10,... | collective-permute-start | bytes 196616 | tf_op jit(solution)/shard_map/ppermute | solution.py:293
  65.0 2.4 %collective-permute-start.5 = (bf16[4,128,128]{2,1,0:T(8,128)(2,1)S(1)}, bf16[4,128,128]{2,1,0:T(8,128)(2,1)S(1)}, u32[]{:S(2)}, u32[]{:S(2)}) collective-permute-start(bf16[4,128,128]{2,1,0:T(8,128)(2,1)S(1)} %get-tuple-element.34), channel_id=1, source_target_pairs={{0,2},{2,4},{4,6},{6,8},{8,10},{10,12},{12,14},{1,3},{3,5},{5,7},{... | collective-permute-start | bytes 393224 | tf_op jit(solution)/shard_map/ppermute | solution.py:290
  67.3 1.3 %collective-permute-start.6 = (bf16[4,128,128]{2,1,0:T(8,128)(2,1)S(1)}, bf16[4,128,128]{2,1,0:T(8,128)(2,1)S(1)}, u32[]{:S(2)}, u32[]{:S(2)}) collective-permute-start(bf16[4,128,128]{2,1,0:T(8,128)(2,1)S(1)} %get-tuple-element.35), channel_id=1, source_target_pairs={{2,0},{4,2},{6,4},{8,6},{10,8},{12,10},{14,12},{3,1},{5,3},{7,5},{... | collective-permute-start | bytes 393224 | tf_op jit(solution)/shard_map/ppermute | solution.py:291
  68.6 0.0 collective-permute-done.12
  68.6 3.7 %collective-permute-start.13 = (f32[162,128]{1,0:T(8,128)S(1)}, f32[162,128]{1,0:T(8,128)S(1)}, u32[]{:S(2)}, u32[]{:S(2)}) collective-permute-start(f32[162,128]{1,0:T(8,128)S(1)} %add.63), channel_id=1, source_target_pairs={{0,8},{2,10},{4,12},{6,14},{8,0},{10,2},{12,4},{14,6},{1,9},{3,11}... | collective-permute-start | bytes 248840 | tf_op jit(solution)/shard_map/ppermute | solution.py:313
  72.4 0.0 collective-permute-done.8.above_side
  72.4 1.3 %collective-permute-start.9 = (bf16[4,64,128]{2,1,0:T(8,128)(2,1)S(1)}, bf16[4,64,128]{2,1,0:T(8,128)(2,1)S(1)}, u32[]{:S(2)}, u32[]{:S(2)}) collective-permute-start(bf16[4,64,128]{2,1,0:T(8,128)(2,1)S(1)} %get-tuple-element.38), channel_id=1, source_target_pairs={{2,1},{3,0},{4,3},{5,2},{6,5},{7,4},{8,7},{9,6},{10,9},{11,8},{12,... | collective-permute-start | bytes 196616 | tf_op jit(solution)/shard_map/ppermute | solution.py:294
  73.7 5.0 %collective-permute-done.9.below_side = bf16[4,64,128]{2,1,0:T(8,128)(2,1)S(1)} collective-permute-done((bf16[4,64,128]{2,1,0:T(8,128)(2,1)S(1)}, bf16[4,64,128]{2,1,0:T(8,128)(2,1)S(1)}, u32[]{:S(2)}, u32[]{:S(2)}) %collective-permute-start.9) | collective-permute-done | bytes 65568 | tf_op jit(solution)/shard_map/ppermute | solution.py:294
  78.7 0.0 collective-permute-done.5.above
  78.7 0.0 collective-permute-done.6.below
  78.7 0.0 collective-permute-done.7.side
  78.7 2.1 %shard_map.105 = bf16[2,96,1024]{2,1,0:T(8,128)(2,1)} custom-call(bf16[2,256,256]{2,1,0:T(8,128)(2,1)S(1)} %pad_maximum_fusion.perm, s32[1]{0:T(128)} %bitcast.7.left_ref, s32[2]{0:T(128)S(1)} %copy-done.6, f32[4,512,128]{2,1,0:T(8,128)S(1)} %get-tuple-element.33.centre, bf16[4,128,128]{2,1,0:T(8,128)(2,1)S(1)} %collective-permute-done.5.above, ...), custom_call_target="tpu_custom_call" | custom-call | tf_op jit(solution)/shard_map/pallas_call | solution.py:339
  80.8 0.0 collective-permute-done.13
  80.8 0.7 add_multiply_fusion
  (6 shorter events, 0.1 us)
Async XLA Ops:
  0.6 25.5 %copy-start.4 = (s32[32]{0:T(128)S(1)}, s32[32]{0:T(128)}, u32[]{:S(2)}) copy-start(s32[32]{0:T(128)} %owner.1) | copy-start | bytes 388
  0.8 1.0 %copy-start = (bf16[2,128,1024]{2,1,0:T(8,128)(2,1)S(1)}, bf16[2,128,1024]{2,1,0:T(8,128)(2,1)}, u32[]{:S(2)}) copy-start(bf16[2,128,1024]{2,1,0:T(8,128)(2,1)} %cot.1) | copy-start | bytes 1572868
  1.9 1.0 %copy-start.1 = (bf16[2,96,1024]{2,1,0:T(8,128)(2,1)S(1)}, bf16[2,96,1024]{2,1,0:T(8,128)(2,1)}, u32[]{:S(2)}) copy-start(bf16[2,96,1024]{2,1,0:T(8,128)(2,1)} %earlier.1) | copy-start | bytes 1179652
  2.9 1.0 %copy-start.2 = (bf16[2,96,1024]{2,1,0:T(8,128)(2,1)S(1)}, bf16[2,96,1024]{2,1,0:T(8,128)(2,1)}, u32[]{:S(2)}) copy-start(bf16[2,96,1024]{2,1,0:T(8,128)(2,1)} %later.1) | copy-start | bytes 1179652
  3.9 0.7 copy-start.3
  4.5 0.7 copy-start.5
  5.2 0.7 copy-start.7
  8.8 21.7 %collective-permute-start.3 = (bf16[4,64,128]{2,1,0:T(8,128)(2,1)}, bf16[4,64,128]{2,1,0:T(8,128)(2,1)}, u32[]{:S(2)}, u32[]{:S(2)}) collective-permute-start(bf16[4,64,128]{2,1,0:T(8,128)(2,1)} %get-tuple-element.25), channel_id=1, source_target_pairs={{0,3},{1,2},{2,5},{3,4},{4,7},{5,6},{6,9},{7,8},{8,11},{9,10},{10,... | collective-permute-start | bytes 196616 | tf_op jit(solution)/shard_map/ppermute | solution.py:293
  13.9 16.6 %collective-permute-start.4 = (bf16[4,64,128]{2,1,0:T(8,128)(2,1)}, bf16[4,64,128]{2,1,0:T(8,128)(2,1)}, u32[]{:S(2)}, u32[]{:S(2)}) collective-permute-start(bf16[4,64,128]{2,1,0:T(8,128)(2,1)} %get-tuple-element.26), channel_id=1, source_target_pairs={{2,1},{3,0},{4,3},{5,2},{6,5},{7,4},{8,7},{9,6},{10,9},{11,8},{12,... | collective-permute-start | bytes 196616 | tf_op jit(solution)/shard_map/ppermute | solution.py:294
  15.2 15.4 %collective-permute-start.2 = (bf16[4,256,128]{2,1,0:T(8,128)(2,1)}, bf16[4,256,128]{2,1,0:T(8,128)(2,1)}, u32[]{:S(2)}, u32[]{:S(2)}) collective-permute-start(bf16[4,256,128]{2,1,0:T(8,128)(2,1)} %get-tuple-element.24), channel_id=1, source_target_pairs={{0,1},{1,0},{2,3},{3,2},{4,5},{5,4},{6,7},{7,6},{8,9},{9,8},{10,11... | collective-permute-start | bytes 786440 | tf_op jit(solution)/shard_map/ppermute | solution.py:292
  16.0 14.6 %collective-permute-start.1 = (bf16[4,128,128]{2,1,0:T(8,128)(2,1)}, bf16[4,128,128]{2,1,0:T(8,128)(2,1)S(1)}, u32[]{:S(2)}, u32[]{:S(2)}) collective-permute-start(bf16[4,128,128]{2,1,0:T(8,128)(2,1)} %get-tuple-element.40), channel_id=1, source_target_pairs={{2,0},{4,2},{6,4},{8,6},{10,8},{12,10},{14,12},{3,1},{5,3},{7,5},{... | collective-permute-start | bytes 393224 | tf_op jit(solution)/shard_map/ppermute | solution.py:291
  17.3 13.3 %collective-permute-start = (bf16[4,128,128]{2,1,0:T(8,128)(2,1)}, bf16[4,128,128]{2,1,0:T(8,128)(2,1)}, u32[]{:S(2)}, u32[]{:S(2)}) collective-permute-start(bf16[4,128,128]{2,1,0:T(8,128)(2,1)} %get-tuple-element.41), channel_id=1, source_target_pairs={{0,2},{2,4},{4,6},{6,8},{8,10},{10,12},{12,14},{1,3},{3,5},{5,7},{... | collective-permute-start | bytes 393224 | tf_op jit(solution)/shard_map/ppermute | solution.py:290
  30.5 11.4 %copy-start.6 = (s32[2]{0:T(128)S(1)}, s32[2]{0:T(128)}, u32[]{:S(2)}) copy-start(s32[2]{0:T(128)} %mask.5) | copy-start | bytes 28
  41.5 13.7 %collective-permute-start.10 = (f32[162,128]{1,0:T(8,128)S(1)}, f32[162,128]{1,0:T(8,128)S(1)}, u32[]{:S(2)}, u32[]{:S(2)}) collective-permute-start(f32[162,128]{1,0:T(8,128)S(1)} %get-tuple-element.39), channel_id=1, source_target_pairs={{0,1},{1,0},{2,3},{3,2},{4,5},{5,4},{6,7},{7,6},{8,9},{9,8},{10,11... | collective-permute-start | bytes 248840 | tf_op jit(solution)/shard_map/ppermute | solution.py:310
  55.0 23.7 %collective-permute-start.7 = (bf16[4,256,128]{2,1,0:T(8,128)(2,1)S(1)}, bf16[4,256,128]{2,1,0:T(8,128)(2,1)S(1)}, u32[]{:S(2)}, u32[]{:S(2)}) collective-permute-start(bf16[4,256,128]{2,1,0:T(8,128)(2,1)S(1)} %get-tuple-element.36), channel_id=1, source_target_pairs={{0,1},{1,0},{2,3},{3,2},{4,5},{5,4},{6,7},{7,6},{8,9},{9,8},{10,11... | collective-permute-start | bytes 786440 | tf_op jit(solution)/shard_map/ppermute | solution.py:292
  55.2 4.3 %collective-permute-start.11 = (f32[162,128]{1,0:T(8,128)S(1)}, f32[162,128]{1,0:T(8,128)S(1)}, u32[]{:S(2)}, u32[]{:S(2)}) collective-permute-start(f32[162,128]{1,0:T(8,128)S(1)} %add.61), channel_id=1, source_target_pairs={{0,2},{2,0},{4,6},{6,4},{8,10},{10,8},{12,14},{14,12},{1,3},{3,1},... | collective-permute-start | bytes 248840 | tf_op jit(solution)/shard_map/ppermute | solution.py:313
  59.6 9.0 %collective-permute-start.12 = (f32[162,128]{1,0:T(8,128)S(1)}, f32[162,128]{1,0:T(8,128)S(1)}, u32[]{:S(2)}, u32[]{:S(2)}) collective-permute-start(f32[162,128]{1,0:T(8,128)S(1)} %add.62), channel_id=1, source_target_pairs={{0,4},{2,6},{4,0},{6,2},{8,12},{10,14},{12,8},{14,10},{1,5},{3,7},... | collective-permute-start | bytes 248840 | tf_op jit(solution)/shard_map/ppermute | solution.py:313
  60.0 12.3 %collective-permute-start.8 = (bf16[4,64,128]{2,1,0:T(8,128)(2,1)S(1)}, bf16[4,64,128]{2,1,0:T(8,128)(2,1)S(1)}, u32[]{:S(2)}, u32[]{:S(2)}) collective-permute-start(bf16[4,64,128]{2,1,0:T(8,128)(2,1)S(1)} %get-tuple-element.37), channel_id=1, source_target_pairs={{0,3},{1,2},{2,5},{3,4},{4,7},{5,6},{6,9},{7,8},{8,11},{9,10},{10,... | collective-permute-start | bytes 196616 | tf_op jit(solution)/shard_map/ppermute | solution.py:293
  65.0 13.7 %collective-permute-start.5 = (bf16[4,128,128]{2,1,0:T(8,128)(2,1)S(1)}, bf16[4,128,128]{2,1,0:T(8,128)(2,1)S(1)}, u32[]{:S(2)}, u32[]{:S(2)}) collective-permute-start(bf16[4,128,128]{2,1,0:T(8,128)(2,1)S(1)} %get-tuple-element.34), channel_id=1, source_target_pairs={{0,2},{2,4},{4,6},{6,8},{8,10},{10,12},{12,14},{1,3},{3,5},{5,7},{... | collective-permute-start | bytes 393224 | tf_op jit(solution)/shard_map/ppermute | solution.py:290
  67.3 11.4 %collective-permute-start.6 = (bf16[4,128,128]{2,1,0:T(8,128)(2,1)S(1)}, bf16[4,128,128]{2,1,0:T(8,128)(2,1)S(1)}, u32[]{:S(2)}, u32[]{:S(2)}) collective-permute-start(bf16[4,128,128]{2,1,0:T(8,128)(2,1)S(1)} %get-tuple-element.35), channel_id=1, source_target_pairs={{2,0},{4,2},{6,4},{8,6},{10,8},{12,10},{14,12},{3,1},{5,3},{7,5},{... | collective-permute-start | bytes 393224 | tf_op jit(solution)/shard_map/ppermute | solution.py:291
  68.6 12.2 %collective-permute-start.13 = (f32[162,128]{1,0:T(8,128)S(1)}, f32[162,128]{1,0:T(8,128)S(1)}, u32[]{:S(2)}, u32[]{:S(2)}) collective-permute-start(f32[162,128]{1,0:T(8,128)S(1)} %add.63), channel_id=1, source_target_pairs={{0,8},{2,10},{4,12},{6,14},{8,0},{10,2},{12,4},{14,6},{1,9},{3,11}... | collective-permute-start | bytes 248840 | tf_op jit(solution)/shard_map/ppermute | solution.py:313
  72.4 6.3 %collective-permute-start.9 = (bf16[4,64,128]{2,1,0:T(8,128)(2,1)S(1)}, bf16[4,64,128]{2,1,0:T(8,128)(2,1)S(1)}, u32[]{:S(2)}, u32[]{:S(2)}) collective-permute-start(bf16[4,64,128]{2,1,0:T(8,128)(2,1)S(1)} %get-tuple-element.38), channel_id=1, source_target_pairs={{2,1},{3,0},{4,3},{5,2},{6,5},{7,4},{8,7},{9,6},{10,9},{11,8},{12,... | collective-permute-start | bytes 196616 | tf_op jit(solution)/shard_map/ppermute | solution.py:294
